TPU v7x, 32 devices: a whole 2x2x4 slice. The times are simulated.
32 devices in a mesh: seq: 4 (over z), tp: 2 (over y), rep: 4 (over x, core).
Axes of the slice: x: 2, y: 2, z: 4, core: 2. Of those that a mesh axis runs over, the one named last changes fastest.
Arguments:
- counts: int32 [4, 4], P('rep'), may hold values from 1 to 160, 256 in all within a row
- prompt_of: int32 [4, 256], P('rep'), may hold values from 0 to 7, as said below
- queries: bfloat16 [4, 640, 8192], P('rep', 'seq', 'tp'), may hold values from -10 to 10
- new_kv: bfloat16 [4, 640, 2, 1024], P('rep', 'seq', None, 'tp'), may hold values from -10 to 10
- prompt_keys: bfloat16 [4, 8, 4096, 1024], P('rep', None, 'seq', 'tp'), may hold values from -6 to 6
- prompt_values: bfloat16 [4, 8, 4096, 1024], P('rep', None, 'seq', 'tp'), may hold values from -6 to 6
- suffix_keys: bfloat16 [4, 256, 64, 1024], P('rep', 'seq', None, 'tp'), may hold values from -9 to 9
- suffix_values: bfloat16 [4, 256, 64, 1024], P('rep', 'seq', None, 'tp'), may hold values from -6 to 6
- gen_len: int32 [4, 256], P('rep', 'seq'), may hold values from 1 to 64, 8192 in all within a row
- out_weight: bfloat16 [8192, 8192], P('tp', ('seq', 'rep')), may hold values from -0.0625 to 0.0625
Outputs:
- projected: bfloat16 [1024, 8192], P('tp', ('seq', 'rep'))
Inputs may be any that keep to these rules, and one draw needn't show every extreme that they name: In each group the live slots of seq index s are its first counts[s] slots; together they hold the group's rows in order. `prompt_of`: in each group every prompt is named by exactly 32 rows.
All inputs are finite; a program needn't handle non-finite values. No bound on the sum of `gen_len` on one device may be relied on, other than what follows from the above.
Results may differ from a plain program's by a relative error of at most 0.014.
Values may be sent and summed in bfloat16 or wider, within the bound.
A program may use at most 128 MiB of HBM per device.

v0:
```python
import jax
import jax.numpy as jnp
from jax import lax
from jax.sharding import PartitionSpec as P

HD = 128


def body(
    counts,
    prompt_of,
    queries,
    new_kv,
    prompt_keys,
    prompt_values,
    suffix_keys,
    suffix_values,
    gen_len,
    out_weight,
):
    seq_count = lax.axis_size("seq")
    seq_index = lax.axis_index("seq")
    capacity = queries.shape[1]
    width = queries.shape[2]
    kv_width = new_kv.shape[3]
    kv_local = kv_width // HD
    q_local = width // HD
    share = q_local // kv_local
    per_device = gen_len.shape[1]
    group_rows = per_device * seq_count
    prompt_count = prompt_keys.shape[1]
    block_rows = group_rows // prompt_count
    scale = HD ** (-0.5)
    tally = counts[0]
    ends = jnp.cumsum(tally)
    starts = ends - tally
    row_ids = jnp.arange(group_rows, dtype=jnp.int32)
    holder = jnp.sum((ends[None, :] <= row_ids[:, None]).astype(jnp.int32), axis=1)
    devices = jnp.arange(seq_count, dtype=jnp.int32)
    first_row = jnp.sum(jnp.where(holder[:, None] == devices[None, :], starts[None, :], 0), axis=1)
    slot_of_row = holder * capacity + row_ids - first_row
    slot_queries, slot_kv = (
        lax.all_gather(queries[0], "seq", axis=0, tiled=True),
        lax.all_gather(new_kv[0].reshape(capacity, 2 * kv_width), "seq", axis=0, tiled=True),
    )
    picker = (
        slot_of_row[:, None] == jnp.arange(seq_count * capacity, dtype=jnp.int32)[None, :]
    ).astype(jnp.bfloat16)
    row_queries = jnp.dot(picker, slot_queries, preferred_element_type=jnp.float32).astype(
        jnp.bfloat16
    )
    own_picker = lax.dynamic_slice_in_dim(picker, seq_index * per_device, per_device, 0)
    own_kv = jnp.dot(own_picker, slot_kv, preferred_element_type=jnp.float32).astype(jnp.bfloat16)
    grouped = row_queries.reshape(group_rows, kv_local, share, HD)
    row_order = jnp.argsort(prompt_of[0], stable=True)

    def prompt_step(index, carry):
        best, total, mixed = carry
        rows = lax.dynamic_slice_in_dim(row_order, index * block_rows, block_rows, 0)
        block_queries = jnp.take(grouped, rows, axis=0)
        keys = lax.dynamic_index_in_dim(prompt_keys[0], index, 0, keepdims=False).reshape(
            -1, kv_local, HD
        )
        values = lax.dynamic_index_in_dim(prompt_values[0], index, 0, keepdims=False).reshape(
            -1, kv_local, HD
        )
        scores = (
            jnp.einsum("rkgd,nkd->rkgn", block_queries, keys, preferred_element_type=jnp.float32)
            * scale
        )
        peak = jnp.max(scores, axis=-1)
        weights = jnp.exp(scores - peak[..., None])
        mass = jnp.sum(weights, axis=-1)
        blended = jnp.einsum(
            "rkgn,nkd->rkgd",
            weights.astype(jnp.bfloat16),
            values,
            preferred_element_type=jnp.float32,
        )
        best = best.at[rows].set(peak.reshape(block_rows, q_local))
        total = total.at[rows].set(mass.reshape(block_rows, q_local))
        mixed = mixed.at[rows].set(blended.reshape(block_rows, width))
        return (best, total, mixed)

    start_state = (
        jnp.zeros((group_rows, q_local), jnp.float32),
        jnp.zeros((group_rows, q_local), jnp.float32),
        jnp.zeros((group_rows, width), jnp.float32),
    )
    partial_value = lax.fori_loop(0, prompt_count, prompt_step, start_state)
    got_best, got_total, got_mixed = (
        lax.all_to_all(partial_value[0], "seq", split_axis=0, concat_axis=0, tiled=True),
        lax.all_to_all(partial_value[1], "seq", split_axis=0, concat_axis=0, tiled=True),
        lax.all_to_all(partial_value[2], "seq", split_axis=0, concat_axis=0, tiled=True),
    )
    got_best = got_best.reshape(seq_count, per_device, q_local)
    best = jnp.max(got_best, axis=0)
    factor = jnp.exp(got_best - best[None])
    total = jnp.sum(got_total.reshape(seq_count, per_device, q_local) * factor, axis=0)
    mixed = jnp.sum(
        got_mixed.reshape(seq_count, per_device, width) * jnp.repeat(factor, HD, axis=-1), axis=0
    )
    mine = lax.dynamic_slice_in_dim(row_queries, seq_index * per_device, per_device, 0).reshape(
        per_device, kv_local, share, HD
    )
    cache_keys = suffix_keys[0].reshape(per_device, -1, kv_local, HD)
    cache_values = suffix_values[0].reshape(per_device, -1, kv_local, HD)
    suffix_scores = (
        jnp.einsum("rkgd,rskd->rkgs", mine, cache_keys, preferred_element_type=jnp.float32) * scale
    )
    live = jnp.arange(cache_keys.shape[1], dtype=jnp.int32)[None, :] < gen_len[0][:, None]
    suffix_scores = jnp.where(live[:, None, None, :], suffix_scores, -jnp.inf)
    fresh_keys = own_kv[:, :kv_width].reshape(per_device, kv_local, HD)
    fresh_values = own_kv[:, kv_width:].reshape(per_device, kv_local, HD)
    self_score = (
        jnp.einsum("rkgd,rkd->rkg", mine, fresh_keys, preferred_element_type=jnp.float32) * scale
    )
    prior = best.reshape(per_device, kv_local, share)
    peak = jnp.maximum(jnp.maximum(prior, jnp.max(suffix_scores, axis=-1)), self_score)
    carry_factor = jnp.exp(prior - peak)
    suffix_weights = jnp.exp(suffix_scores - peak[..., None])
    self_weight = jnp.exp(self_score - peak)
    mass = (
        total.reshape(per_device, kv_local, share) * carry_factor
        + jnp.sum(suffix_weights, axis=-1)
        + self_weight
    )
    blended = mixed.reshape(per_device, kv_local, share, HD) * carry_factor[..., None]
    blended = blended + jnp.einsum(
        "rkgs,rskd->rkgd",
        suffix_weights.astype(jnp.bfloat16),
        cache_values,
        preferred_element_type=jnp.float32,
    )
    blended = (
        blended
        + self_weight.astype(jnp.bfloat16).astype(jnp.float32)[..., None]
        * fresh_values.astype(jnp.float32)[:, :, None, :]
    )
    attended = (blended / mass[..., None]).reshape(per_device, width).astype(jnp.bfloat16)
    group_block = lax.all_gather(attended, "seq", axis=0, tiled=True)
    every_row = lax.all_gather(group_block, "rep", axis=0, tiled=True)
    summed = lax.psum_scatter(
        jnp.dot(every_row, out_weight, preferred_element_type=jnp.float32).astype(jnp.bfloat16),
        "tp",
        scatter_dimension=0,
        tiled=True,
    )
    return summed


def solution(mesh):
    in_specs = (
        P("rep", None),
        P("rep", None),
        P("rep", "seq", "tp"),
        P("rep", "seq", None, "tp"),
        P("rep", None, "seq", "tp"),
        P("rep", None, "seq", "tp"),
        P("rep", "seq", None, "tp"),
        P("rep", "seq", None, "tp"),
        P("rep", "seq"),
        P("tp", ("seq", "rep")),
    )
    out_specs = P("tp", ("seq", "rep"))
    return jax.shard_map(body, mesh=mesh, in_specs=in_specs, out_specs=out_specs, check_vma=False)
```

profile of v0, /device:TPU:1, one launch (start us, length us, event | category | flops | bytes accessed | tf_op | source)
XLA Modules:
  0.0 572.8 jit_solution(15710172238060762840)
XLA Ops:
  8.1 3.8 sort.17
  12.8 96.5 %all-gather.12.cloned.1.call-done = bf16[1,640,4096]{2,1,0:T(8,128)(2,1)} async-done(((bf16[1,160,4096]{2,1,0:T(8,128)(2,1)}), bf16[1,640,4096]{2,1,0:T(8,128)(2,1)}) %all-gather.12.cloned.1.call-update) | async-done | bytes 5242896 | tf_op jit(solution)/shard_map/all_gather | solution.py:43
  109.3 4.3 fusion.18
  118.7 170.8 %while.17 = (s32[]{:T(128)}, f32[256,32]{1,0:T(8,128)S(1)}, f32[256,32]{1,0:T(8,128)}, f32[256,4096]{1,0:T(8,128)}, s32[256]{0:T(256)S(1)}, /*index=5*/bf16[1,8,...) while((s32[]{:T(128)}, f32[256,32]{1,0:T(8,128)S(1)}, ...), condition=%wide.region_10.11_spmd, body=%wide.region_4.10_spmd.sunk | while | flops 545389760 | bytes 30995492 | solution.py:90
  129.9 5.3 scatter_custom_fusion.11
  135.3 3.1 fusion.72
  151.3 5.3 scatter_custom_fusion.11
  156.6 3.1 fusion.72
  172.6 5.3 scatter_custom_fusion.11
  178.0 3.1 fusion.72
  194.0 5.3 scatter_custom_fusion.11
  215.3 5.3 scatter_custom_fusion.11
  220.6 3.1 fusion.72
  236.7 5.3 scatter_custom_fusion.11
  242.0 3.1 fusion.72
  258.0 5.3 scatter_custom_fusion.11
  279.4 5.3 scatter_custom_fusion.11
  290.3 3.3 all-to-all-start.1
  294.6 3.4 all-to-all-done.1
  298.0 6.9 %all_to_all.27 = f32[4,1,2048]{2,1,0:T(1,128)S(1)} all-to-all(f32[4,1,2048]{2,1,0:T(1,128)S(1)} %reshape.193), channel_id=1, replica_groups=mesh['seq'=4,'tp'=2,'rep'=4] {'seq'}, dimensions={0} | all-to-all | bytes 65536 | tf_op jit(solution)/shard_map/all_to_all | solution.py:93
  304.9 5.0 all-to-all-start
  311.0 6.9 %reshape_squeeze.9 = bf16[64,64,4,128]{3,2,1,0:T(4,128)(2,1)} reshape(bf16[1,64,64,512]{3,2,1,0:T(8,128)(2,1)} %param.18) | data formatting | bytes 8388608 | tf_op jit(solution)/shard_map/reshape;squeeze | solution.py:106
  317.9 7.0 %reshape_squeeze.11 = bf16[64,64,4,128]{3,2,1,0:T(4,128)(2,1)} reshape(bf16[1,64,64,512]{3,2,1,0:T(8,128)(2,1)} %param.19) | data formatting | bytes 8388608 | tf_op jit(solution)/shard_map/reshape;squeeze | solution.py:107
  325.1 44.0 %all-gather.6.cloned.1.call-done = bf16[640,1024]{1,0:T(8,128)(2,1)} async-done(((bf16[160,1024]{1,0:T(8,128)(2,1)}), bf16[640,1024]{1,0:T(8,128)(2,1)}) %all-gather.6.cloned.1.call-update) | async-done | bytes 1310736 | tf_op jit(solution)/shard_map/all_gather | solution.py:44
  372.6 4.6 fusion.52
  383.5 5.0 reshape.139
  388.5 35.1 %all-to-all-done = f32[4,64,4096]{2,1,0:T(8,128)} async-done(((f32[4,64,4096]{2,1,0:T(8,128)}), f32[4,64,4096]{2,1,0:T(8,128)}, u32[]{:S(2)}, u32[]{:S(2)}) %all-to-all-start) | async-done | bytes 4194336 | tf_op jit(solution)/shard_map/all_to_all | solution.py:94
  423.6 4.3 multiply_reduce_fusion
  431.3 45.9 %all-gather.8.cloned.1.call-done = bf16[256,4096]{1,0:T(8,128)(2,1)} async-done(((bf16[64,4096]{1,0:T(8,128)(2,1)}), bf16[256,4096]{1,0:T(8,128)(2,1)}) %all-gather.8.cloned.1.call-update) | async-done | bytes 2097168 | tf_op jit(solution)/shard_map/all_gather | solution.py:141
  477.2 58.8 %all-gather.10.cloned.1.call-done = bf16[1024,4096]{1,0:T(8,128)(2,1)} async-done(((bf16[256,4096]{1,0:T(8,128)(2,1)}), bf16[1024,4096]{1,0:T(8,128)(2,1)}) %all-gather.10.cloned.1.call-update) | async-done | bytes 8388624 | tf_op jit(solution)/shard_map/all_gather | solution.py:142
  536.0 10.1 %convolution_convert_fusion = bf16[1024,512]{1,0:T(8,128)(2,1)} fusion(bf16[1024,4096]{1,0:T(8,128)(2,1)} %all-gather.10.cloned.1.call-done, bf16[4096,512]{1,0:T(8,128)(2,1)} %param.21), kind=kOutput, calls=%fused_computation.33 | convolution fusion | flops 4295491584 | bytes 13631488 | tf_op jit(solution)/shard_map/dot_general | solution.py:144
  546.2 20.1 %reduce-scatter.2.cloned.1.call-done = bf16[512,512]{1,0:T(8,128)(2,1)} async-done(((bf16[1024,512]{1,0:T(8,128)(2,1)}), bf16[512,512]{1,0:T(8,128)(2,1)}) %reduce-scatter.2.cloned.1.call-update) | async-done | bytes 524304 | tf_op jit(solution)/shard_map/reduce_scatter | solution.py:143
  (211 shorter events, 135.4 us)
Async XLA Ops:
  6.5 102.7 %all-gather.12.cloned.1.call-start = ((), (), s32[]{:S(2)}) async-start(), calls=%async_computation.8 | async-start | bytes 6553600 | tf_op jit(solution)/shard_map/all_gather | solution.py:43
  113.6 4.4 copy-start.3
  129.9 8.5 %copy-start = (f32[256,32]{1,0:T(8,128)S(1)}, f32[256,32]{1,0:T(8,128)}, u32[]{:S(2)}) copy-start(f32[256,32]{1,0:T(8,128)} %get-tuple-element.306) | copy-start | bytes 98308 | tf_op jit(solution)/shard_map/while
  139.2 0.8 copy-start.1
  151.3 8.5 %copy-start = (f32[256,32]{1,0:T(8,128)S(1)}, f32[256,32]{1,0:T(8,128)}, u32[]{:S(2)}) copy-start(f32[256,32]{1,0:T(8,128)} %get-tuple-element.306) | copy-start | bytes 98308 | tf_op jit(solution)/shard_map/while
  160.5 0.8 copy-start.1
  172.6 8.5 %copy-start = (f32[256,32]{1,0:T(8,128)S(1)}, f32[256,32]{1,0:T(8,128)}, u32[]{:S(2)}) copy-start(f32[256,32]{1,0:T(8,128)} %get-tuple-element.306) | copy-start | bytes 98308 | tf_op jit(solution)/shard_map/while
  181.9 0.8 copy-start.1
  193.9 8.5 %copy-start = (f32[256,32]{1,0:T(8,128)S(1)}, f32[256,32]{1,0:T(8,128)}, u32[]{:S(2)}) copy-start(f32[256,32]{1,0:T(8,128)} %get-tuple-element.306) | copy-start | bytes 98308 | tf_op jit(solution)/shard_map/while
  203.2 0.8 copy-start.1
  215.3 8.5 %copy-start = (f32[256,32]{1,0:T(8,128)S(1)}, f32[256,32]{1,0:T(8,128)}, u32[]{:S(2)}) copy-start(f32[256,32]{1,0:T(8,128)} %get-tuple-element.306) | copy-start | bytes 98308 | tf_op jit(solution)/shard_map/while
  224.6 0.8 copy-start.1
  236.6 8.5 %copy-start = (f32[256,32]{1,0:T(8,128)S(1)}, f32[256,32]{1,0:T(8,128)}, u32[]{:S(2)}) copy-start(f32[256,32]{1,0:T(8,128)} %get-tuple-element.306) | copy-start | bytes 98308 | tf_op jit(solution)/shard_map/while
  245.9 0.8 copy-start.1
  258.0 8.5 %copy-start = (f32[256,32]{1,0:T(8,128)S(1)}, f32[256,32]{1,0:T(8,128)}, u32[]{:S(2)}) copy-start(f32[256,32]{1,0:T(8,128)} %get-tuple-element.306) | copy-start | bytes 98308 | tf_op jit(solution)/shard_map/while
  267.3 0.8 copy-start.1
  279.3 8.5 %copy-start = (f32[256,32]{1,0:T(8,128)S(1)}, f32[256,32]{1,0:T(8,128)}, u32[]{:S(2)}) copy-start(f32[256,32]{1,0:T(8,128)} %get-tuple-element.306) | copy-start | bytes 98308 | tf_op jit(solution)/shard_map/while
  288.6 0.8 copy-start.1
  290.3 7.7 %all-to-all-start.1 = ((f32[4,1,2048]{2,1,0:T(1,128)}), f32[4,1,2048]{2,1,0:T(1,128)S(1)}, u32[]{:S(2)}, u32[]{:S(2)}) async-start(f32[4,1,2048]{2,1,0:T(1,128)} %reshape.191), calls=%async_computation.1 | async-start | bytes 65536 | tf_op jit(solution)/shard_map/all_to_all | solution.py:92
  304.9 5.1 copy-start.4
  304.9 118.8 %all-to-all-start = ((f32[4,64,4096]{2,1,0:T(8,128)}), f32[4,64,4096]{2,1,0:T(8,128)}, u32[]{:S(2)}, u32[]{:S(2)}) async-start(f32[4,64,4096]{2,1,0:T(8,128)} %bitcast.141), calls=%async_computation | async-start | bytes 8388608 | tf_op jit(solution)/shard_map/all_to_all | solution.py:94
  309.9 59.3 %all-gather.6.cloned.1.call-start = ((), (), s32[]{:S(2)}) async-start(), calls=%async_computation.4 | async-start | bytes 1638400 | tf_op jit(solution)/shard_map/all_gather | solution.py:44
  310.7 166.5 %all-gather.8.cloned.1.call-start = ((), (), s32[]{:S(2)}) async-start(), calls=%async_computation.5 | async-start | bytes 2621440 | tf_op jit(solution)/shard_map/all_gather | solution.py:141
  317.9 7.0 %copy-start.5 = (s32[1,64]{1,0:T(1,128)S(1)}, s32[1,64]{1,0:T(1,128)}, u32[]{:S(2)}) copy-start(s32[1,64]{1,0:T(1,128)} %param.20) | copy-start | bytes 772
  423.6 4.6 copy-start.2
  431.3 104.8 %all-gather.10.cloned.1.call-start = ((), (), s32[]{:S(2)}) async-start(), calls=%async_computation.6 | async-start | bytes 10485760 | tf_op jit(solution)/shard_map/all_gather | solution.py:142
  477.2 89.1 %reduce-scatter.2.cloned.1.call-start = ((), (), s32[]{:S(2)}) async-start(), calls=%async_computation.7 | async-start | bytes 1572864 | tf_op jit(solution)/shard_map/reduce_scatter | solution.py:143
Sparse Core Ops, SparseCore 0:
  8.9 100.3 all-gather.11
  312.3 56.8 all-gather.5
  431.4 45.7 all-gather.7
  478.6 57.4 all-gather.9
  546.3 19.8 reduce-scatter.1
where the time goes:
time: 575 us; the launch traced here: 573 us
  waiting for transfers between devices  305 us (53%)
  local copies, waits for them, and re-layouts  131 us (23%)
  matrix products  68.7 us (12%)
  other arithmetic  38.7 us (7%)
  between operations  13.4 us (2%)
  starting transfers between devices  8.6 us (1%)
  blocking collectives  6.85 us (1%)
    all_gather x1, waiting for transfers between devices, body(): lax.all_gather(queries[0], 'seq', axis=0, tiled=True)  96.5 us
    all_gather x1, waiting for transfers between devices, body(): every_row = lax.all_gather(group_block, 'rep', axis=0, tiled=True)  58.8 us
    all_gather x1, waiting for transfers between devices, body(): group_block = lax.all_gather(attended, 'seq', axis=0, tiled=True)  45.9 us
    all_gather x1, waiting for transfers between devices, body(): lax.all_gather(new_kv[0].reshape(capacity, 2 * kv_width), 'seq', axis=0,...  44 us
    scatter x8, local copies, waits for them, and re-layouts, prompt_step(): mixed = mixed.at[rows].set(blended.reshape(block_rows, width))  42.7 us
    all_to_all x1, waiting for transfers between devices, body(): lax.all_to_all(partial_value[2], 'seq', split_axis=0, concat_axis=0, tile...  35.1 us
    reduce_sum x8, other arithmetic, prompt_step(): mass = jnp.sum(weights, axis=-1)  24.7 us
    dot_general x8, matrix products, prompt_step(): jnp.einsum('rkgn,nkd->rkgd', weights.astype(jnp.bfloat16), values, prefer...  24.5 us
  transfers between devices with their start and end apart: 7, of which 7 were waited for; matrix products, arithmetic and copies ran while one was open for 7% of the time, Pallas kernels for 0%

commit v1 on v0

v1 whole, which is shorter than its diff:
```python
import functools

import jax
import jax.numpy as jnp
from jax import lax
from jax.experimental import pallas as pl
from jax.experimental.pallas import tpu as pltpu
from jax.sharding import PartitionSpec as P

HD = 128
CHUNK = 512
SUF_ROWS = 16
NEG = -1e30
MESH = pl.DeviceIdType.MESH
VMEM_LIMIT = 48 * 1024 * 1024
F32 = jnp.float32
BF16 = jnp.bfloat16


def signal(**where):
    pl.semaphore_signal(
        pltpu.get_barrier_semaphore(), inc=1, device_id=where, device_id_type=MESH
    )


def greet_line(me, n):
    @pl.when(me > 0)
    def _():
        signal(seq=me - 1)

    @pl.when(me < n - 1)
    def _():
        signal(seq=me + 1)


def await_greetings(me, n, others=0):
    line = jnp.minimum(me, 1) + jnp.minimum(n - 1 - me, 1)
    pl.semaphore_wait(pltpu.get_barrier_semaphore(), line + others)


def remote(src, dst, send, recv, **where):
    return pltpu.make_async_remote_copy(
        src_ref=src, dst_ref=dst, send_sem=send, recv_sem=recv, device_id=where, device_id_type=MESH
    )


def spread_kernel(n, pick_ref, q_ref, out_ref, mine, from_left, from_right, to_right, to_left,
                  send_r, recv_r, send_l, recv_l):
    me = lax.axis_index("seq")
    chunks = mine.shape[0]
    if n > 1:
        greet_line(me, n)
    for c in range(chunks):
        mine[c] = jnp.dot(
            pick_ref[...], q_ref[:, c * CHUNK:(c + 1) * CHUNK], preferred_element_type=F32
        ).astype(BF16)
    if n == 1:
        out_ref[...] = mine[...]
        return
    await_greetings(me, n)

    def right(c):
        return remote(to_right.at[c], from_left.at[c], send_r.at[c], recv_r.at[c], seq=me + 1)

    def left(c):
        return remote(to_left.at[c], from_right.at[c], send_l.at[c], recv_l.at[c], seq=me - 1)

    def step(t, carry):
        c = t - me

        @pl.when((c >= 0) & (c < chunks))
        def _():
            @pl.when(me == 0)
            def _():
                to_right[c] = mine[c]

            @pl.when(me > 0)
            def _():
                right(c).wait_recv()
                to_right[c] = from_left[c] + mine[c]

            @pl.when(me < n - 1)
            def _():
                right(c).start()

        e = t - (n - 1 - me)

        @pl.when((e >= 0) & (e < chunks))
        def _():
            @pl.when(me == n - 1)
            def _():
                to_left[e] = mine[e]

            @pl.when(me < n - 1)
            def _():
                left(e).wait_recv()
                to_left[e] = from_right[e] + mine[e]

            @pl.when(me > 0)
            def _():
                left(e).start()

        return carry

    lax.fori_loop(0, chunks + n - 1, step, 0)

    def finish(c, carry):
        @pl.when(me < n - 1)
        def _():
            out_ref[c] = to_right[c] + from_right[c]
            right(c).wait_send()

        @pl.when(me == n - 1)
        def _():
            out_ref[c] = to_right[c]

        @pl.when(me > 0)
        def _():
            left(c).wait_send()

        return carry

    lax.fori_loop(0, chunks, finish, 0)


def prompt_kernel(share, q_ref, k_ref, v_ref, nk_ref, nv_ref, held_ref, o_ref, lse_ref):
    per = CHUNK // HD
    rows = q_ref.shape[1]
    scale = HD ** (-0.5)
    q = jnp.concatenate(
        [q_ref[g // per, :, (g % per) * HD:(g % per + 1) * HD] for g in range(share)], axis=0
    )
    s = lax.dot_general(
        q, k_ref[0], (((1,), (1,)), ((), ())), preferred_element_type=F32
    ) * scale
    nk = jnp.concatenate([nk_ref[...].astype(F32)] * share, axis=0)
    nv = jnp.concatenate([nv_ref[...].astype(F32)] * share, axis=0)
    held = jnp.concatenate([held_ref[...]] * share, axis=0)
    fresh = jnp.sum(q.astype(F32) * nk, axis=1, keepdims=True) * scale
    fresh = jnp.where(held > 0.5, fresh, NEG)
    m = jnp.maximum(jnp.max(s, axis=1, keepdims=True), fresh)
    w = jnp.exp(s - m)
    wn = jnp.exp(fresh - m)
    total = jnp.sum(w, axis=1, keepdims=True) + wn
    o = jnp.dot(w.astype(BF16), v_ref[0], preferred_element_type=F32)
    o = o + wn.astype(BF16).astype(F32) * nv
    o = (o / total).astype(BF16)
    lse = m + jnp.log(total)
    for g in range(share):
        o_ref[:, g * HD:(g + 1) * HD] = o[g * rows:(g + 1) * rows]
    lse_ref[0] = jnp.concatenate([lse[g * rows:(g + 1) * rows] for g in range(share)], axis=1)


def combine_kernel(n, kv_local, share, o_ref, s_ref, q_ref, k_ref, v_ref, len_ref, out_ref,
                   got_o, got_s, suf_o, suf_s, send_o, recv_o, send_s, recv_s):
    me = lax.axis_index("seq")
    rows = q_ref.shape[0]
    span = k_ref.shape[1]
    heads = kv_local * share
    scale = HD ** (-0.5)
    copies = []
    if n > 1:
        for off in range(1, n):
            signal(seq=(me + off) % n)
        pl.semaphore_wait(pltpu.get_barrier_semaphore(), n - 1)
    for off in range(1, n):
        peer = (me + off) % n
        i = off - 1
        copies.append(remote(s_ref.at[peer], got_s.at[i], send_s.at[i], recv_s.at[i], seq=peer))
        copies.append(remote(o_ref.at[peer], got_o.at[i], send_o.at[i], recv_o.at[i], seq=peer))
    for copy in copies:
        copy.start()

    tall, wide = share * SUF_ROWS, SUF_ROWS * span
    at = lax.broadcasted_iota(jnp.int32, (tall, wide), 1)
    own_row = lax.broadcasted_iota(jnp.int32, (tall, wide), 0) % SUF_ROWS
    offset = at - own_row * span

    def suffix(b, carry):
        block = pl.ds(pl.multiple_of(b * SUF_ROWS, SUF_ROWS), SUF_ROWS)
        lens = jnp.concatenate([len_ref[block, :]] * share, axis=0)
        live = (offset >= 0) & (offset < lens)
        found = []
        for h in range(kv_local):
            q = jnp.concatenate(
                [q_ref[block, (h * share + g) * HD:(h * share + g + 1) * HD] for g in range(share)],
                axis=0,
            )
            k = k_ref[block, :, h * HD:(h + 1) * HD].reshape(wide, HD)
            v = v_ref[block, :, h * HD:(h + 1) * HD].reshape(wide, HD)
            s = lax.dot_general(
                q, k, (((1,), (1,)), ((), ())), preferred_element_type=F32
            ) * scale
            s = jnp.where(live, s, NEG)
            m = jnp.max(s, axis=1, keepdims=True)
            w = jnp.exp(s - m)
            total = jnp.sum(w, axis=1, keepdims=True)
            o = jnp.dot(w.astype(BF16), v, preferred_element_type=F32) / total
            lse = m + jnp.log(total)
            for g in range(share):
                part = slice(g * SUF_ROWS, (g + 1) * SUF_ROWS)
                suf_o[block, (h * share + g) * HD:(h * share + g + 1) * HD] = o[part]
                found.append(lse[part])
        if heads < HD:
            found.append(jnp.zeros((SUF_ROWS, HD - heads), F32))
        suf_s[block, :] = jnp.concatenate(found, axis=1)
        return carry

    lax.fori_loop(0, rows // SUF_ROWS, suffix, 0)
    for copy in copies:
        copy.wait()

    stats = [suf_s[...], s_ref[me]] + [got_s[i] for i in range(n - 1)]
    best = functools.reduce(jnp.maximum, stats)
    weights = [jnp.exp(one - best) for one in stats]
    total = functools.reduce(jnp.add, weights)
    weights = [one / total for one in weights]
    for h in range(heads):
        cols = slice(h * HD, (h + 1) * HD)
        mixed = weights[0][:, h:h + 1] * suf_o[:, cols]
        mixed = mixed + weights[1][:, h:h + 1] * o_ref[me, :, cols].astype(F32)
        for i in range(n - 1):
            mixed = mixed + weights[2 + i][:, h:h + 1] * got_o[i, :, cols].astype(F32)
        out_ref[:, cols] = mixed.astype(BF16)


def project_kernel(n, reps, tps, att_ref, w_ref, out_ref, every, parts, got, own,
                   send_r, recv_r, send_l, recv_l, send_x, recv_x, send_t, recv_t, own_sem):
    me, rep, tp = lax.axis_index("seq"), lax.axis_index("rep"), lax.axis_index("tp")
    distances = []
    d = reps // 2
    while d >= 1:
        distances.append(d)
        d //= 2

    def across(r, d):
        return r + d - 2 * d * ((r // d) % 2)

    if n > 1:
        greet_line(me, n)
    for d in distances:
        signal(rep=across(rep, d))
    for off in range(1, tps):
        signal(tp=(tp + off) % tps)
    local = pltpu.make_async_copy(att_ref, every.at[rep * n + me], own_sem)
    local.start()
    local.wait()
    await_greetings(me, n, len(distances) + tps - 1)

    def right(j):
        place = every.at[rep * n + j]
        return remote(place, place, send_r.at[j], recv_r.at[j], seq=me + 1)

    def left(j):
        place = every.at[rep * n + j]
        return remote(place, place, send_l.at[j], recv_l.at[j], seq=me - 1)

    def over(stage, r, j):
        place = every.at[r * n + j]
        return remote(place, place, send_x.at[stage, r * n + j], recv_x.at[r * n + j],
                      rep=across(rep, distances[stage]))

    def hop(t, carry):
        j = me - t

        @pl.when(j >= 0)
        def _():
            @pl.when(t > 0)
            def _():
                right(j).wait_recv()

            @pl.when(me < n - 1)
            def _():
                right(j).start()

            for stage in range(len(distances)):
                over(stage, rep, j).start()

        e = me + t

        @pl.when(e < n)
        def _():
            @pl.when(t > 0)
            def _():
                left(e).wait_recv()
                for stage in range(len(distances)):
                    over(stage, rep, e).start()

            @pl.when(me > 0)
            def _():
                left(e).start()

        return carry

    lax.fori_loop(0, n, hop, 0)

    held = [rep]
    for stage in range(len(distances)):
        arrived = [across(r, distances[stage]) for r in held]
        for r in arrived:
            def pass_on(j, carry, r=r, stage=stage):
                over(stage, r, j).wait_recv()
                for later in range(stage + 1, len(distances)):
                    over(later, r, j).start()
                return carry

            lax.fori_loop(0, n, pass_on, 0)
        held = held + arrived

    blocks, tall = every.shape[0], every.shape[1]
    share = blocks // tps
    unit = min(share, max(1, 256 // tall))

    def rows_of(peer, put):
        def piece(u, carry):
            x = every[pl.ds(peer * share + u * unit, unit)].reshape(unit * tall, -1)
            y = jnp.dot(x, w_ref[...], preferred_element_type=F32)
            put(pl.ds(pl.multiple_of(u * unit * tall, unit * tall), unit * tall), y)
            return carry

        lax.fori_loop(0, share // unit, piece, 0)

    sums = []
    for off in range(1, tps):
        peer = (tp + off) % tps
        i = off - 1

        def put(where, y, i=i):
            parts[i, where, :] = y.astype(BF16)

        rows_of(peer, put)
        copy = remote(parts.at[i], got.at[i], send_t.at[i], recv_t.at[i], tp=peer)
        copy.start()
        sums.append(copy)

    def put_own(where, y):
        own[where, :] = y

    rows_of(tp, put_own)
    for copy in sums:
        copy.wait()
    result = own[...]
    for i in range(tps - 1):
        result = result + got[i].astype(F32)
    out_ref[...] = result.astype(BF16)

    def drain(j, carry):
        @pl.when((j <= me) & (me < n - 1))
        def _():
            right(j).wait_send()

        @pl.when((j >= me) & (me > 0))
        def _():
            left(j).wait_send()

        return carry

    lax.fori_loop(0, n, drain, 0)
    held = [rep]
    for stage in range(len(distances)):
        for r in held:
            def sent(j, carry, r=r, stage=stage):
                over(stage, r, j).wait_send()
                return carry

            lax.fori_loop(0, n, sent, 0)
        held = held + [across(r, distances[stage]) for r in held]


def params(number):
    return pltpu.CompilerParams(
        collective_id=number, has_side_effects=True, vmem_limit_bytes=VMEM_LIMIT
    )


def vmem():
    return pl.BlockSpec(memory_space=pltpu.VMEM)


def body(
    counts,
    prompt_of,
    queries,
    new_kv,
    prompt_keys,
    prompt_values,
    suffix_keys,
    suffix_values,
    gen_len,
    out_weight,
):
    n = lax.axis_size("seq")
    reps = lax.axis_size("rep")
    tps = lax.axis_size("tp")
    me = lax.axis_index("seq")
    capacity, width = queries.shape[1:]
    kv_width = new_kv.shape[3]
    kv_local = kv_width // HD
    heads = width // HD
    share = heads // kv_local
    per_device = gen_len.shape[1]
    group_rows = per_device * n
    prompts, positions = prompt_keys.shape[1:3]
    block_rows = group_rows // prompts
    chunks = width // CHUNK

    tally = counts[0]
    start = jnp.sum(jnp.where(jnp.arange(n, dtype=jnp.int32) < me, tally, 0))
    count = jnp.sum(jnp.where(jnp.arange(n, dtype=jnp.int32) == me, tally, 0))
    row_ids = jnp.arange(group_rows, dtype=jnp.int32)
    of = prompt_of[0]
    before = (of[None, :] < of[:, None]) | (
        (of[None, :] == of[:, None]) & (row_ids[None, :] < row_ids[:, None])
    )
    rank = jnp.sum(before.astype(jnp.int32), axis=1)
    place = (rank[None, :] == row_ids[:, None]).astype(BF16)
    back = (rank[:, None] == row_ids[None, :]).astype(BF16)
    row_of = jnp.sum(jnp.where(rank[None, :] == row_ids[:, None], row_ids[None, :], 0), axis=1)
    slot = row_of - start
    mine = (slot >= 0) & (slot < count)
    picker = (
        (slot[:, None] == jnp.arange(capacity, dtype=jnp.int32)[None, :]) & mine[:, None]
    ).astype(BF16)
    fresh = jnp.dot(
        picker, new_kv[0].reshape(capacity, 2 * kv_width), preferred_element_type=F32
    ).astype(BF16)
    held = mine.astype(F32)[:, None]

    chunk_shape = (chunks, group_rows, CHUNK)
    sorted_q = pl.pallas_call(
        functools.partial(spread_kernel, n),
        out_shape=jax.ShapeDtypeStruct(chunk_shape, BF16),
        in_specs=[vmem(), vmem()],
        out_specs=vmem(),
        scratch_shapes=[pltpu.VMEM(chunk_shape, BF16)] * 5
        + [pltpu.SemaphoreType.DMA((chunks,))] * 4,
        compiler_params=params(0),
        name="spread_queries",
    )(picker, queries[0])

    per = share * HD // CHUNK
    partial_o, lse = pl.pallas_call(
        functools.partial(prompt_kernel, share),
        grid=(kv_local, prompts),
        out_shape=(
            jax.ShapeDtypeStruct((group_rows, width), BF16),
            jax.ShapeDtypeStruct((kv_local, group_rows, share), F32),
        ),
        in_specs=[
            pl.BlockSpec((per, block_rows, CHUNK), lambda h, p: (h, p, 0)),
            pl.BlockSpec((1, positions, HD), lambda h, p: (p, 0, h)),
            pl.BlockSpec((1, positions, HD), lambda h, p: (p, 0, h)),
            pl.BlockSpec((block_rows, HD), lambda h, p: (p, h)),
            pl.BlockSpec((block_rows, HD), lambda h, p: (p, h + kv_local)),
            pl.BlockSpec((block_rows, 1), lambda h, p: (p, 0)),
        ],
        out_specs=(
            pl.BlockSpec((block_rows, share * HD), lambda h, p: (p, h)),
            pl.BlockSpec((1, block_rows, share), lambda h, p: (h, p, 0)),
        ),
        compiler_params=pltpu.CompilerParams(vmem_limit_bytes=VMEM_LIMIT),
        name="prompt_attention",
    )(sorted_q, prompt_keys[0], prompt_values[0], fresh, fresh, held)

    row_o = jnp.dot(back, partial_o, preferred_element_type=F32).astype(BF16)
    row_s = jnp.take(jnp.swapaxes(lse, 0, 1).reshape(group_rows, heads), rank, axis=0)
    row_s = jnp.pad(row_s, ((0, 0), (0, HD - heads)))
    own_back = lax.dynamic_slice_in_dim(back, me * per_device, per_device, 0)
    own_q = jnp.einsum("rp,cpw->rcw", own_back, sorted_q, preferred_element_type=F32)
    own_q = own_q.astype(BF16).reshape(per_device, width)

    attended = pl.pallas_call(
        functools.partial(combine_kernel, n, kv_local, share),
        out_shape=jax.ShapeDtypeStruct((per_device, width), BF16),
        in_specs=[vmem()] * 6,
        out_specs=vmem(),
        scratch_shapes=[
            pltpu.VMEM((max(1, n - 1), per_device, width), BF16),
            pltpu.VMEM((max(1, n - 1), per_device, HD), F32),
            pltpu.VMEM((per_device, width), F32),
            pltpu.VMEM((per_device, HD), F32),
        ]
        + [pltpu.SemaphoreType.DMA((max(1, n - 1),))] * 4,
        compiler_params=params(1),
        name="exchange_and_suffix",
    )(
        row_o.reshape(n, per_device, width),
        row_s.reshape(n, per_device, HD),
        own_q,
        suffix_keys[0],
        suffix_values[0],
        gen_len[0][:, None],
    )

    columns = out_weight.shape[1]
    out_rows = group_rows * reps // tps
    stages = max(1, reps.bit_length() - 1)
    dma = pltpu.SemaphoreType.DMA
    return pl.pallas_call(
        functools.partial(project_kernel, n, reps, tps),
        out_shape=jax.ShapeDtypeStruct((out_rows, columns), BF16),
        in_specs=[vmem()] * 2,
        out_specs=vmem(),
        scratch_shapes=[
            pltpu.VMEM((reps * n, per_device, width), BF16),
            pltpu.VMEM((max(1, tps - 1), out_rows, columns), BF16),
            pltpu.VMEM((max(1, tps - 1), out_rows, columns), BF16),
            pltpu.VMEM((out_rows, columns), F32),
            dma((n,)), dma((n,)), dma((n,)), dma((n,)),
            dma((stages, reps * n)), dma((reps * n,)),
            dma((max(1, tps - 1),)), dma((max(1, tps - 1),)),
            pltpu.SemaphoreType.DMA,
        ],
        compiler_params=params(2),
        name="gather_and_project",
    )(attended, out_weight)


def solution(mesh):
    in_specs = (
        P("rep", None),
        P("rep", None),
        P("rep", "seq", "tp"),
        P("rep", "seq", None, "tp"),
        P("rep", None, "seq", "tp"),
        P("rep", None, "seq", "tp"),
        P("rep", "seq", None, "tp"),
        P("rep", "seq", None, "tp"),
        P("rep", "seq"),
        P("tp", ("seq", "rep")),
    )
    out_specs = P("tp", ("seq", "rep"))
    return jax.shard_map(body, mesh=mesh, in_specs=in_specs, out_specs=out_specs, check_vma=False)
```

time: 575 us -> 227 us (0.39)
  waiting for transfers between devices: 305 us -> 0 us
  Pallas kernels: 0 us -> 217 us
  local copies, waits for them, and re-layouts: 131 us -> 3.75 us
  matrix products: 68.7 us -> 1.58 us
  other arithmetic: 38.7 us -> 4.23 us
  between operations: 13.4 us -> 0.17 us
  starting transfers between devices: 8.6 us -> 0 us
  blocking collectives: 6.85 us -> 0 us
    all_gather x4 -> x0, waiting for transfers between devices: 245 us -> none  [the longest x1 96.5 us: body(): lax.all_gather(queries[0], 'seq', axis=0, tiled=True)]
    pallas_call x0 -> x4, Pallas kernels: none -> 217 us  [the longest x1 79 us: body(): pl.pallas_call(functools.partial(project_kernel, n, reps, tps), out_shape...]
    dot_general x22 -> x3, matrix products: 68.7 us -> 1.58 us  [the longest x1 0.76 us: body(): row_o = jnp.dot(back, partial_o, preferred_element_type=F32).astype(BF16)]
    scatter x24 -> x0, local copies, waits for them, and re-layouts: 54.8 us -> none  [the longest x8 42.7 us: prompt_step(): mixed = mixed.at[rows].set(blended.reshape(block_rows, width))]
    all_to_all x2 -> x0, waiting for transfers between devices: 38.5 us -> none  [the longest x1 35.1 us: body(): lax.all_to_all(partial_value[2], 'seq', split_axis=0, concat_axis=0, tile...]
    reduce_sum x13 -> x3, other arithmetic: 30 us -> 2.53 us  [the longest x1 1.48 us: body(): count = jnp.sum(jnp.where(jnp.arange(n, dtype=jnp.int32) == me, tally, 0))]
    dynamic_slice x24 -> x0, local copies, waits for them, and re-layouts: 22 us -> none  [the longest x16 17.7 us: prompt_step(): lax.dynamic_index_in_dim(prompt_values[0], index, 0, keepdims=False)]
    reduce_scatter x1 -> x0, waiting for transfers between devices: 20.1 us -> none  [body(): lax.psum_scatter(jnp.dot(every_row, out_weight, preferred_element_type=jn...]
  transfers between devices with their start and end apart: 7 -> 0, of which waited for: 7 -> 0; matrix products, arithmetic and copies ran while one was open for 7% -> 0% of each run, Pallas kernels for 0% -> 0%
where the time goes in v1:
time: 227 us; the launch traced here: 226 us
  Pallas kernels  217 us (96%)
  other arithmetic  4.23 us (2%)
  local copies, waits for them, and re-layouts  3.75 us (2%)
    pallas_call x1, Pallas kernels, body(): pl.pallas_call(functools.partial(project_kernel, n, reps, tps), out_shape...  79 us
    pallas_call x1, Pallas kernels, body(): pl.pallas_call(functools.partial(spread_kernel, n), out_shape=jax.ShapeDt...  62.6 us
    pallas_call x1, Pallas kernels, body(): pl.pallas_call(functools.partial(combine_kernel, n, kv_local, share), out...  43.6 us
    pallas_call x1, Pallas kernels, body(): pl.pallas_call(functools.partial(prompt_kernel, share), grid=(kv_local, p...  31.6 us

profile of v1, /device:TPU:1, one launch (start us, length us, event | category | flops | bytes accessed | tf_op | source)
XLA Modules:
  0.0 226.5 jit_solution(11980483516300764516)
XLA Ops:
  0.0 0.0 copy-start.1
  0.0 1.5 fusion.11
  1.5 0.9 convert_reduce_fusion
  2.4 0.1 select_reduce_fusion
  2.6 1.3 fusion.13
  3.9 0.7 copy.22.len_ref
  4.7 0.1 iota_compare_fusion.2
  4.8 0.1 copy.18.held_ref
  4.9 0.1 fusion.5.pick_ref
  5.1 1.0 copy.24
  6.1 0.3 convolution_convert_fusion.1.nk_ref.nv_ref
  6.4 0.0 copy-done.1
  6.5 62.6 %spread_queries.1.q_ref = bf16[8,256,512]{2,1,0:T(8,128)(2,1)S(1)} custom-call(bf16[256,160]{1,0:T(8,128)(2,1)S(1)} %fusion.5.pick_ref, bf16[160,4096]{1,0:T(8,128)(2,1)S(1)} %bitcast.31), custom_call_target="tpu_custom_call" | custom-call | tf_op jit(solution)/shard_map/spread_queries/pallas_call | solution.py:430
  69.0 0.5 fusion
  69.5 31.6 %prompt_attention.1 = (bf16[256,4096]{1,0:T(8,128)(2,1)S(1)}, f32[4,256,8]{2,1,0:T(8,128)S(1)}) custom-call(bf16[8,256,512]{2,1,0:T(8,128)(2,1)S(1)} %spread_queries.1.q_ref, bf16[8,1024,512]{2,1,0:T(8,128)(2,1)} %bitcast.34, bf16[8,1024,512]{2,1,0:T(8,128)(2,1)} %bitcast.35, bf16[256,1024]{1,0:T(8,128)(2,1)S(1)} %convolution_convert_fusion.1.nk_ref.nv_ref, ...), custom_call_target="tpu_custom_call" | custom-call | tf_op jit(solution)/shard_map/prompt_attention/pallas_call | solution.py:442
  101.1 0.8 convolution_convert_fusion
  101.8 0.2 copy.19
  102.0 0.1 copy.23
  102.0 0.1 copy.20
  102.1 0.7 gather_fusion
  102.9 0.1 broadcast_select_fusion
  103.0 0.0 copy-start
  103.0 43.6 %exchange_and_suffix.1.att_ref = bf16[64,4096]{1,0:T(8,128)(2,1)S(1)} custom-call(bf16[4,64,4096]{2,1,0:T(8,128)(2,1)S(1)} %bitcast.29, f32[4,64,128]{2,1,0:T(8,128)S(1)} %bitcast.32, bf16[64,4096]{1,0:T(8,128)(2,1)S(1)} %bitcast.30, bf16[64,64,512]{2,1,0:T(8,128)(2,1)} %bitcast.36, bf16[64,64,512]{2,1,0:T(8,128)(2,1)} %bitcast.37, s32[64,1]{1,0:T(8,128)S(1)} %copy.22.len_ref), custom_call_target="tpu_custom_call" | custom-call | tf_op jit(solution)/shard_map/exchange_and_suffix/pallas_call | solution.py:472
  146.7 0.0 copy-done
  146.7 79.0 %gather_and_project.1 = bf16[512,512]{1,0:T(8,128)(2,1)S(1)} custom-call(bf16[64,4096]{1,0:T(8,128)(2,1)S(1)} %exchange_and_suffix.1.att_ref, bf16[4096,512]{1,0:T(8,128)(2,1)S(1)} %copy-done), custom_call_target="tpu_custom_call" | custom-call | tf_op jit(solution)/shard_map/gather_and_project/pallas_call | solution.py:499
  225.7 0.8 copy.28
  (4 shorter events, 0.0 us)
Async XLA Ops:
  0.0 6.4 %copy-start.1 = (bf16[1,160,4096]{2,1,0:T(8,128)(2,1)S(1)}, bf16[1,160,4096]{2,1,0:T(8,128)(2,1)}, u32[]{:S(2)}) copy-start(bf16[1,160,4096]{2,1,0:T(8,128)(2,1)} %param.12) | copy-start | bytes 3932164
  103.0 43.7 %copy-start = (bf16[4096,512]{1,0:T(8,128)(2,1)S(1)}, bf16[4096,512]{1,0:T(8,128)(2,1)}, u32[]{:S(2)}) copy-start(bf16[4096,512]{1,0:T(8,128)(2,1)} %w_ref.1) | copy-start | bytes 12582916

commit v2 on v1

--- a/solution.py
+++ b/solution.py
@@ -8,7 +8,9 @@
 from jax.sharding import PartitionSpec as P
 
 HD = 128
-CHUNK = 512
+CHUNK = 256
+PROMPTS_STEP = 4
+LOG2E = 1.4426950408889634
 SUF_ROWS = 16
 NEG = -1e30
 MESH = pl.DeviceIdType.MESH
@@ -125,30 +127,37 @@
 
 def prompt_kernel(share, q_ref, k_ref, v_ref, nk_ref, nv_ref, held_ref, o_ref, lse_ref):
     per = CHUNK // HD
-    rows = q_ref.shape[1]
-    scale = HD ** (-0.5)
-    q = jnp.concatenate(
-        [q_ref[g // per, :, (g % per) * HD:(g % per + 1) * HD] for g in range(share)], axis=0
-    )
-    s = lax.dot_general(
-        q, k_ref[0], (((1,), (1,)), ((), ())), preferred_element_type=F32
-    ) * scale
-    nk = jnp.concatenate([nk_ref[...].astype(F32)] * share, axis=0)
-    nv = jnp.concatenate([nv_ref[...].astype(F32)] * share, axis=0)
-    held = jnp.concatenate([held_ref[...]] * share, axis=0)
-    fresh = jnp.sum(q.astype(F32) * nk, axis=1, keepdims=True) * scale
-    fresh = jnp.where(held > 0.5, fresh, NEG)
-    m = jnp.maximum(jnp.max(s, axis=1, keepdims=True), fresh)
-    w = jnp.exp(s - m)
-    wn = jnp.exp(fresh - m)
-    total = jnp.sum(w, axis=1, keepdims=True) + wn
-    o = jnp.dot(w.astype(BF16), v_ref[0], preferred_element_type=F32)
-    o = o + wn.astype(BF16).astype(F32) * nv
-    o = (o / total).astype(BF16)
-    lse = m + jnp.log(total)
-    for g in range(share):
-        o_ref[:, g * HD:(g + 1) * HD] = o[g * rows:(g + 1) * rows]
-    lse_ref[0] = jnp.concatenate([lse[g * rows:(g + 1) * rows] for g in range(share)], axis=1)
+    prompts = k_ref.shape[0]
+    rows = q_ref.shape[1] // prompts
+    factor = HD ** (-0.5) * LOG2E
+    every = range(prompts)
+    spans = [slice(i * rows, (i + 1) * rows) for i in every]
+    q = [
+        jnp.concatenate(
+            [q_ref[g // per, one, (g % per) * HD:(g % per + 1) * HD] for g in range(share)], axis=0
+        )
+        for one in spans
+    ]
+    for i, one in enumerate(spans):
+        s = lax.dot_general(q[i], k_ref[i], (((1,), (1,)), ((), ())), preferred_element_type=F32)
+        nk = jnp.concatenate([nk_ref[one, :].astype(F32)] * share, axis=0)
+        nv = jnp.concatenate([nv_ref[one, :].astype(F32)] * share, axis=0)
+        held = jnp.concatenate([held_ref[one, :]] * share, axis=0)
+        fresh = jnp.sum(q[i].astype(F32) * nk, axis=1, keepdims=True)
+        fresh = jnp.where(held > 0.5, fresh, NEG)
+        m = jnp.maximum(jnp.max(s, axis=1, keepdims=True), fresh)
+        w = jnp.exp2((s - m) * factor)
+        wn = jnp.exp2((fresh - m) * factor)
+        total = jnp.sum(w, axis=1, keepdims=True) + wn
+        o = jnp.dot(w.astype(BF16), v_ref[i], preferred_element_type=F32)
+        o = o + wn.astype(BF16).astype(F32) * nv
+        o = (o / total).astype(BF16)
+        lse = m * HD ** (-0.5) + jnp.log(total)
+        for g in range(share):
+            o_ref[one, g * HD:(g + 1) * HD] = o[g * rows:(g + 1) * rows]
+        lse_ref[0, one, :] = jnp.concatenate(
+            [lse[g * rows:(g + 1) * rows] for g in range(share)], axis=1
+        )
 
 
 def combine_kernel(n, kv_local, share, o_ref, s_ref, q_ref, k_ref, v_ref, len_ref, out_ref,
@@ -315,30 +324,33 @@
         def piece(u, carry):
             x = every[pl.ds(peer * share + u * unit, unit)].reshape(unit * tall, -1)
             y = jnp.dot(x, w_ref[...], preferred_element_type=F32)
-            put(pl.ds(pl.multiple_of(u * unit * tall, unit * tall), unit * tall), y)
+            put(u, pl.ds(pl.multiple_of(u * unit * tall, unit * tall), unit * tall), y)
             return carry
 
         lax.fori_loop(0, share // unit, piece, 0)
 
-    sums = []
+    def swap(i, peer, u):
+        where = pl.ds(pl.multiple_of(u * unit * tall, unit * tall), unit * tall)
+        return remote(parts.at[i, where], got.at[i, where], send_t.at[i, u], recv_t.at[i, u],
+                      tp=peer)
+
     for off in range(1, tps):
         peer = (tp + off) % tps
         i = off - 1
 
-        def put(where, y, i=i):
+        def put(u, where, y, i=i, peer=peer):
             parts[i, where, :] = y.astype(BF16)
+            swap(i, peer, u).start()
 
         rows_of(peer, put)
-        copy = remote(parts.at[i], got.at[i], send_t.at[i], recv_t.at[i], tp=peer)
-        copy.start()
-        sums.append(copy)
-
-    def put_own(where, y):
+
+    def put_own(u, where, y):
         own[where, :] = y
 
     rows_of(tp, put_own)
-    for copy in sums:
-        copy.wait()
+    for off in range(1, tps):
+        for u in range(share // unit):
+            swap(off - 1, (tp + off) % tps, u).wait()
     result = own[...]
     for i in range(tps - 1):
         result = result + got[i].astype(F32)
@@ -439,24 +451,26 @@
     )(picker, queries[0])
 
     per = share * HD // CHUNK
+    at_once = PROMPTS_STEP if prompts % PROMPTS_STEP == 0 else 1
+    step_rows = at_once * block_rows
     partial_o, lse = pl.pallas_call(
         functools.partial(prompt_kernel, share),
-        grid=(kv_local, prompts),
+        grid=(kv_local, prompts // at_once),
         out_shape=(
             jax.ShapeDtypeStruct((group_rows, width), BF16),
             jax.ShapeDtypeStruct((kv_local, group_rows, share), F32),
         ),
         in_specs=[
-            pl.BlockSpec((per, block_rows, CHUNK), lambda h, p: (h, p, 0)),
-            pl.BlockSpec((1, positions, HD), lambda h, p: (p, 0, h)),
-            pl.BlockSpec((1, positions, HD), lambda h, p: (p, 0, h)),
-            pl.BlockSpec((block_rows, HD), lambda h, p: (p, h)),
-            pl.BlockSpec((block_rows, HD), lambda h, p: (p, h + kv_local)),
-            pl.BlockSpec((block_rows, 1), lambda h, p: (p, 0)),
+            pl.BlockSpec((per, step_rows, CHUNK), lambda h, p: (h, p, 0)),
+            pl.BlockSpec((at_once, positions, HD), lambda h, p: (p, 0, h)),
+            pl.BlockSpec((at_once, positions, HD), lambda h, p: (p, 0, h)),
+            pl.BlockSpec((step_rows, HD), lambda h, p: (p, h)),
+            pl.BlockSpec((step_rows, HD), lambda h, p: (p, h + kv_local)),
+            pl.BlockSpec((step_rows, 1), lambda h, p: (p, 0)),
         ],
         out_specs=(
-            pl.BlockSpec((block_rows, share * HD), lambda h, p: (p, h)),
-            pl.BlockSpec((1, block_rows, share), lambda h, p: (h, p, 0)),
+            pl.BlockSpec((step_rows, share * HD), lambda h, p: (p, h)),
+            pl.BlockSpec((1, step_rows, share), lambda h, p: (h, p, 0)),
         ),
         compiler_params=pltpu.CompilerParams(vmem_limit_bytes=VMEM_LIMIT),
         name="prompt_attention",
@@ -508,7 +522,7 @@
             pltpu.VMEM((out_rows, columns), F32),
             dma((n,)), dma((n,)), dma((n,)), dma((n,)),
             dma((stages, reps * n)), dma((reps * n,)),
-            dma((max(1, tps - 1),)), dma((max(1, tps - 1),)),
+            dma((max(1, tps - 1), reps * n)), dma((max(1, tps - 1), reps * n)),
             pltpu.SemaphoreType.DMA,
         ],
         compiler_params=params(2),

time: 227 us -> 221 us (0.974)
  Pallas kernels: 217 us -> 211 us
    pallas_call x1, Pallas kernels: 31.6 us -> 22.9 us  [body(): pl.pallas_call(functools.partial(prompt_kernel, share), grid=(kv_local, p...]
    pallas_call x1, Pallas kernels: 62.6 us -> 66.5 us  [body(): pl.pallas_call(functools.partial(spread_kernel, n), out_shape=jax.ShapeDt...]
where the time goes in v2:
time: 221 us; the launch traced here: 220 us
  Pallas kernels  211 us (95%)
  other arithmetic  4.23 us (2%)
  local copies, waits for them, and re-layouts  3.74 us (2%)
    pallas_call x1, Pallas kernels, body(): pl.pallas_call(functools.partial(project_kernel, n, reps, tps), out_shape...  77.6 us
    pallas_call x1, Pallas kernels, body(): pl.pallas_call(functools.partial(spread_kernel, n), out_shape=jax.ShapeDt...  66.5 us
    pallas_call x1, Pallas kernels, body(): pl.pallas_call(functools.partial(combine_kernel, n, kv_local, share), out...  43.7 us
    pallas_call x1, Pallas kernels, body(): pl.pallas_call(functools.partial(prompt_kernel, share), grid=(kv_local, p...  22.9 us

profile of v2, /device:TPU:1, one launch (start us, length us, event | category | flops | bytes accessed | tf_op | source)
XLA Modules:
  0.0 220.4 jit_solution(14376911415878533015)
XLA Ops:
  0.0 0.0 copy-start.1
  0.0 1.5 fusion.11
  1.5 0.9 convert_reduce_fusion
  2.4 0.1 select_reduce_fusion
  2.6 1.3 fusion.13
  3.9 0.7 copy.22.len_ref
  4.7 0.1 iota_compare_fusion.2
  4.8 0.1 copy.18.held_ref
  4.9 0.1 fusion.5.pick_ref
  5.1 1.0 copy.24
  6.1 0.3 convolution_convert_fusion.1.nk_ref.nv_ref
  6.4 0.0 copy-done.1
  6.5 66.5 %spread_queries.1.q_ref = bf16[16,256,256]{2,1,0:T(8,128)(2,1)S(1)} custom-call(bf16[256,160]{1,0:T(8,128)(2,1)S(1)} %fusion.5.pick_ref, bf16[160,4096]{1,0:T(8,128)(2,1)S(1)} %bitcast.31), custom_call_target="tpu_custom_call" | custom-call | tf_op jit(solution)/shard_map/spread_queries/pallas_call | solution.py:442
  73.0 0.5 fusion
  73.5 22.9 %prompt_attention.1 = (bf16[256,4096]{1,0:T(8,128)(2,1)S(1)}, f32[4,256,8]{2,1,0:T(8,128)S(1)}) custom-call(bf16[16,256,256]{2,1,0:T(8,128)(2,1)S(1)} %spread_queries.1.q_ref, bf16[8,1024,512]{2,1,0:T(8,128)(2,1)} %bitcast.34, bf16[8,1024,512]{2,1,0:T(8,128)(2,1)} %bitcast.35, bf16[256,1024]{1,0:T(8,128)(2,1)S(1)} %convolution_convert_fusion.1.nk_ref.nv_ref, ...), custom_call_target="tpu_custom_call" | custom-call | tf_op jit(solution)/shard_map/prompt_attention/pallas_call | solution.py:456
  96.4 0.8 convolution_convert_fusion
  97.1 0.2 copy.19
  97.3 0.1 copy.20
  97.4 0.7 gather_fusion
  98.2 0.1 broadcast_select_fusion
  98.3 0.0 copy-start
  98.3 43.7 %exchange_and_suffix.1.att_ref = bf16[64,4096]{1,0:T(8,128)(2,1)S(1)} custom-call(bf16[4,64,4096]{2,1,0:T(8,128)(2,1)S(1)} %bitcast.29, f32[4,64,128]{2,1,0:T(8,128)S(1)} %bitcast.32, bf16[64,4096]{1,0:T(8,128)(2,1)S(1)} %bitcast.30, bf16[64,64,512]{2,1,0:T(8,128)(2,1)} %bitcast.36, bf16[64,64,512]{2,1,0:T(8,128)(2,1)} %bitcast.37, s32[64,1]{1,0:T(8,128)S(1)} %copy.22.len_ref), custom_call_target="tpu_custom_call" | custom-call | tf_op jit(solution)/shard_map/exchange_and_suffix/pallas_call | solution.py:486
  142.0 0.0 copy-done
  142.0 77.6 %gather_and_project.1 = bf16[512,512]{1,0:T(8,128)(2,1)S(1)} custom-call(bf16[64,4096]{1,0:T(8,128)(2,1)S(1)} %exchange_and_suffix.1.att_ref, bf16[4096,512]{1,0:T(8,128)(2,1)S(1)} %copy-done), custom_call_target="tpu_custom_call" | custom-call | tf_op jit(solution)/shard_map/gather_and_project/pallas_call | solution.py:513
  219.6 0.8 copy.28
  (5 shorter events, 0.1 us)
Async XLA Ops:
  0.0 6.4 %copy-start.1 = (bf16[1,160,4096]{2,1,0:T(8,128)(2,1)S(1)}, bf16[1,160,4096]{2,1,0:T(8,128)(2,1)}, u32[]{:S(2)}) copy-start(bf16[1,160,4096]{2,1,0:T(8,128)(2,1)} %param.12) | copy-start | bytes 3932164
  98.3 43.7 %copy-start = (bf16[4096,512]{1,0:T(8,128)(2,1)S(1)}, bf16[4096,512]{1,0:T(8,128)(2,1)}, u32[]{:S(2)}) copy-start(bf16[4096,512]{1,0:T(8,128)(2,1)} %w_ref.1) | copy-start | bytes 12582916
